TPU v7x, 512 devices: a whole 4x8x8 slice. The times are simulated.
512 devices in a mesh: sample: 16 (over z_lo, x), var: 32 (over y, z_hi, core).
Axes of the slice: x: 4, y: 8, z: 8 (z_hi: 2, z_lo: 4; z = z_hi * 4 + z_lo), core: 2. Of those that a mesh axis runs over, the one named last changes fastest.
Arguments:
- data: bfloat16 [12288, 65536], P('sample', 'var'), may hold values from -6 to 6
- test_matrix: bfloat16 [65536, 256], P('var'), may hold values from -6 to 6
Outputs:
- sketch_cov: float32 [65536, 256], P('var', 'sample')
- core_factor: float32 [256, 256], replicated
All inputs are finite; a program needn't handle non-finite values.
Results may differ from a plain program's by a relative error of at most 0.0027.
Values may be sent and summed in bfloat16 or wider, within the bound.
A program may use at most 64 MiB of HBM per device.

v0:
```python
import math

import jax
import jax.numpy as jnp
from jax import lax
from jax.sharding import PartitionSpec as P


def transposed_product(left, right):
    return lax.dot_general(
        left, right, (((0,), (0,)), ((), ())), preferred_element_type=jnp.float32
    )


def precise_product(left, right):
    return lax.dot_general(
        left,
        right,
        (((0,), (0,)), ((), ())),
        precision=lax.Precision.HIGHEST,
        preferred_element_type=jnp.float32,
    )


def per_device(data, test_matrix):
    row_count = data.shape[0]
    var_count = data.shape[1]
    width = test_matrix.shape[1]
    vars_total = var_count * lax.axis_size("var")
    rows_total = row_count * lax.axis_size("sample")
    var_scale = 1.0 / math.sqrt(vars_total)
    row_scale = 1.0 / math.sqrt(rows_total)
    core_scale = 1.0 / math.sqrt(vars_total * rows_total)
    test_wide = test_matrix.astype(jnp.float32)
    term = jnp.dot(data, test_matrix, preferred_element_type=jnp.float32) * var_scale
    sketch = lax.psum(term, "var").astype(jnp.bfloat16)
    cov_part = transposed_product(data, sketch)
    cov_part = cov_part * row_scale
    block = width // lax.axis_size("sample")
    sketch_cov = lax.psum(cov_part, "sample")
    core_term = precise_product(test_wide, sketch_cov) * core_scale
    core = lax.psum(core_term, "var")
    own_cov = lax.dynamic_slice_in_dim(sketch_cov, lax.axis_index("sample") * block, block, 1)
    core = (core + core.T) * 0.5
    core_factor = jnp.linalg.cholesky(core)
    return (own_cov, core_factor)


def solution(mesh):
    return jax.shard_map(
        per_device,
        mesh=mesh,
        in_specs=(P("sample", "var"), P("var", None)),
        out_specs=(P("var", "sample"), P()),
        check_vma=False,
    )
```

profile of v0, /device:TPU:1, one launch (start us, length us, event | category | flops | bytes accessed | tf_op | source)
XLA Modules:
  0.0 772.5 jit_solution(5126788733835124575)
XLA Ops:
  7.2 0.0 copy-start
  7.2 0.0 all-reduce.5.cloned.1.call-start
  7.2 1.8 copy-done
  9.1 3.1 convolution_multiply_fusion.1
  12.1 181.4 %all-reduce.8 = bf16[768,256]{1,0:T(8,128)(2,1)S(1)} all-reduce(f32[768,256]{1,0:T(8,128)} %convolution_multiply_fusion.1), channel_id=1, replica_groups=mesh['sample'=16,'var'=32] {'var'}, use_global_device_ids=true, to_apply=%region_0.0 | all-reduce | flops 196608 | bytes 1179648 | tf_op jit(solution)/shard_map/psum | solution.py:36
  193.5 2.3 fusion
  195.8 0.0 all-reduce.5.cloned.1.call-update
  195.8 0.0 all-reduce.7.cloned.1.call-start
  195.9 172.9 %all-reduce.5.cloned.1.call-done = f32[2048,256]{0,1:T(8,128)} async-done(((f32[2048,256]{0,1:T(8,128)}), f32[2048,256]{0,1:T(8,128)}) %all-reduce.5.cloned.1.call-update) | async-done | bytes 2097168 | tf_op jit(solution)/shard_map/psum | solution.py:40
  368.8 3.6 fusion.1
  372.4 0.0 all-reduce.7.cloned.1.call-update
  372.5 1.6 constant_dynamic-slice_fusion
  374.0 347.9 %all-reduce.7.cloned.1.call-done = f32[256,256]{0,1:T(8,128)} async-done(((f32[256,256]{0,1:T(8,128)}), f32[256,256]{0,1:T(8,128)}) %all-reduce.7.cloned.1.call-update) | async-done | bytes 262160 | tf_op jit(solution)/shard_map/psum | solution.py:42
  722.0 1.8 copy.4
  723.8 1.1 fusion.4
  724.8 0.8 copy.5
  725.7 1.0 fusion.3
  726.7 0.0 copy-start.1
  726.7 0.7 copy-done.1
  727.4 11.7 %cholesky.50 = f32[128,128]{1,0:T(8,128)S(1)} custom-call(f32[128,128]{1,0:T(8,128)S(1)} %cholesky.118), custom_call_target="Cholesky" | custom-call | tf_op jit(solution)/shard_map/jit(cholesky)/cholesky | solution.py:45
  739.1 9.8 %custom-call.11 = f32[1,128,128]{1,2,0:T(8,128)S(1)} custom-call(f32[1,128,128]{2,1,0:T(8,128)S(1)} %get-tuple-element.5), custom_call_target="InvertDiagBlocksLowerTriangular" | custom-call | tf_op jit(solution)/shard_map/jit(cholesky)/cholesky | solution.py:45
  749.0 1.0 constant_dynamic-update-slice_fusion.1
  750.0 1.1 convolution_subtract_fusion
  751.1 11.7 %cholesky.105 = f32[128,128]{1,0:T(8,128)S(1)} custom-call(f32[128,128]{1,0:T(8,128)S(1)} %convolution_subtract_fusion), custom_call_target="Cholesky" | custom-call | tf_op jit(solution)/shard_map/jit(cholesky)/cholesky | solution.py:45
  762.9 0.7 compare_reduce_fusion
  764.9 0.7 select_select_fusion
  (4 shorter events, 0.1 us)
Async XLA Ops:
  7.2 1.9 copy-start
  7.2 361.6 %all-reduce.5.cloned.1.call-start = ((), (), s32[]{:S(2)}) async-start(), calls=%async_computation | async-start | bytes 4194304 | tf_op jit(solution)/shard_map/psum | solution.py:40
  195.8 526.1 %all-reduce.7.cloned.1.call-start = ((), (), s32[]{:S(2)}) async-start(), calls=%async_computation.1 | async-start | bytes 524288 | tf_op jit(solution)/shard_map/psum | solution.py:42
  726.7 0.7 copy-start.1
Sparse Core Ops, SparseCore 0:
  196.0 172.7 all-reduce.4
  372.6 349.3 all-reduce.6
where the time goes:
time: 773 us
  waiting for transfers between devices  521 us (67%)
  blocking collectives  181 us (23%)
  other arithmetic  36.8 us (5%)
  between operations  15.4 us (2%)
  matrix products  11.2 us (1%)
    psum x1, waiting for transfers between devices, per_device(): core = lax.psum(core_term, 'var')  348 us
    psum x1, blocking collectives, per_device(): sketch = lax.psum(term, 'var').astype(jnp.bfloat16)  181 us
    psum x1, waiting for transfers between devices, per_device(): sketch_cov = lax.psum(cov_part, 'sample')  173 us
    another operation x6, other arithmetic, per_device(): core_factor = jnp.linalg.cholesky(core)  34 us
  transfers between devices with their start and end apart: 2, of which 2 were waited for; matrix products, arithmetic and copies ran while one was open for 0% of the time, Pallas kernels for 0%

commit v1 on v0

v1 whole, which is shorter than its diff:
```python
import math

import jax
import jax.numpy as jnp
from jax import lax
from jax.experimental import pallas as pl
from jax.experimental.pallas import tpu as pltpu
from jax.sharding import PartitionSpec as P

MESH = pl.DeviceIdType.MESH
HIGHEST = lax.Precision.HIGHEST
F32 = jnp.float32
BF16 = jnp.bfloat16

NX, NY, NZ = 4, 8, 8
NZL = 4
K = 256
HALF = 128
BLOCK = 16
SLAB = 64


def position():
    s = lax.axis_index("sample")
    v = lax.axis_index("var")
    x = lax.rem(s, NX)
    zl = s // NX
    c = lax.rem(v, 2)
    zh = lax.rem(v // 2, 2)
    y = v // 4
    return x, y, zh * NZL + zl, c


def device(x, y, z, c):
    return (lax.rem(z, NZL) * NX + x, y * 4 + (z // NZL) * 2 + c)


def remote(src, dst, send, recv, target):
    return pltpu.make_async_remote_copy(
        src_ref=src, dst_ref=dst, send_sem=send, recv_sem=recv,
        device_id=target, device_id_type=MESH,
    )


def factor_slab(block, rows, lanes):
    wide = lanes // HALF

    def spread(a):
        return jnp.concatenate([a] * wide, axis=1)

    count = rows // 8
    tiles = [block[8 * t:8 * t + 8, :] for t in range(count)]
    done = []
    row_at = lax.broadcasted_iota(jnp.int32, (8, lanes), 0)
    for t in range(count):
        tile = tiles[t]
        base = 8 * t
        below = range(t + 1, count)
        piv = {}
        for i in range(8):
            for j in range(i + 1):
                piv[i, j] = jnp.broadcast_to(tile[i:i + 1, base + j:base + j + 1], (8, HALF))
        cols = {}
        for u in below:
            for k in range(8):
                cols[u, k] = jnp.broadcast_to(tiles[u][:, base + k:base + k + 1], (8, HALF))
        rowv = [jnp.broadcast_to(tile[i:i + 1, :], (8, lanes)) for i in range(8)]
        for k in range(8):
            inv = lax.rsqrt(piv[k, k])
            rowv[k] = rowv[k] * spread(inv)
            for i in range(k + 1, 8):
                piv[i, k] = piv[i, k] * inv
            for u in below:
                cols[u, k] = cols[u, k] * inv
            for i in range(k + 1, 8):
                for j in range(k + 1, i + 1):
                    piv[i, j] = piv[i, j] - piv[i, k] * piv[j, k]
                rowv[i] = rowv[i] - spread(piv[i, k]) * rowv[k]
                for u in below:
                    cols[u, i] = cols[u, i] - piv[i, k] * cols[u, k]
            for u in below:
                tiles[u] = tiles[u] - spread(cols[u, k]) * rowv[k]
        out = rowv[7]
        for i in range(7):
            out = jnp.where(row_at == i, rowv[i], out)
        done.append(out)
    return jnp.concatenate(done, axis=0)


def kernel(data, test, cov_out, factor_out,
           dv, tv, part, sib, q, yrecv, zsend, zrecv, yown, ysib, sk, skt,
           pm, pxr, px, pzr, pyr, cm, am, um, lm, cv, cvb, cxr, czs, czr, zacc, covv,
           ld, xs, xr, ys, yr, zs, zr, szs, szr, sys_, syr, sbs, sbr, ybs, ybr,
           pxs, pxq, pzs, pzq, pys, pyq, pas, paq, pbs, pbq, pcs, pcq,
           cxs, cxq, czs_s, czq, outs):
    x, y, z, c = position()
    zl = lax.rem(z, NZL)
    zh = z // NZL
    o = 1 - c
    rows = data.shape[0] // NY
    hrows = rows // 2
    nvar = data.shape[1]
    sibling = device(x, y, z, o)

    def ypeer(k):
        return lax.rem(y + k, NY)

    def zpeer(k):
        return lax.rem(z + k, NZ)

    def xpeer(k):
        return lax.rem(x + k, NX)

    def order(i):
        half = (i + 1) // 2
        off = 4 + (1 - 2 * lax.rem(i, 2)) * half
        return lax.rem(y + off, NY)

    tcopy = pltpu.make_async_copy(test, tv, ld.at[NY])
    tcopy.start()

    def dcopy(i):
        r = order(i)
        at = pl.ds(pl.multiple_of(r * rows, rows), rows)
        return pltpu.make_async_copy(data.at[at, :], dv.at[at, :], ld.at[i])

    def start_load(i, carry):
        dcopy(i).start()
        return carry

    lax.fori_loop(0, NY, start_load, 0)

    barrier = pltpu.get_barrier_semaphore()
    peers = [sibling]
    peers += [device(x, ypeer(k), z, c) for k in range(1, NY)]
    peers += [device(x, y, zpeer(k), c) for k in range(1, NZ)]
    peers += [device(xpeer(k), y, z, c) for k in range(1, NX)]
    for p in peers:
        pl.semaphore_signal(barrier, inc=1, device_id=p, device_id_type=MESH)

    tcopy.wait()
    pl.semaphore_wait(barrier, len(peers))

    def sib_copy(r):
        return remote(part.at[o, r], sib.at[r], xs.at[r], xr.at[r], sibling)

    def y_copy(r):
        return remote(q.at[r], yrecv.at[y], ys.at[r], yr.at[y], device(x, r, z, c))

    def sketch_step(i, carry):
        @pl.when(i < NY)
        def _():
            r = order(i)
            dcopy(i).wait()
            at = pl.ds(pl.multiple_of(r * rows, rows), rows)
            p = jnp.dot(dv[at, :], tv[...], preferred_element_type=F32)
            part[0, r] = p[:, :HALF]
            part[1, r] = p[:, HALF:]
            sib_copy(r).start()

        @pl.when(i > 0)
        def _():
            r = order(i - 1)
            sib_copy(r).wait_recv()
            q[r] = part[c, r] + sib[r]

            @pl.when(r != y)
            def _():
                y_copy(r).start()

        return carry

    lax.fori_loop(0, NY + 1, sketch_step, 0)

    total = q[y]
    for k in range(1, NY):
        r = ypeer(k)
        remote(q.at[r], yrecv.at[r], ys.at[r], yr.at[r], device(x, r, z, c)).wait_recv()
        total = total + yrecv[r]
    q[y] = total
    partner = device(x, y, lax.rem(z + NZL, NZ), c)
    other_at = pl.ds(pl.multiple_of((1 - zh) * hrows, hrows), hrows)
    own_at = pl.ds(pl.multiple_of(zh * hrows, hrows), hrows)
    zsend[...] = q[y, other_at, :]
    z_copy = remote(zsend, zrecv, zs, zr, partner)
    z_copy.start()
    z_copy.wait_recv()
    yown[...] = (q[y, own_at, :] + zrecv[...]) * (1.0 / K)
    ysib_copy = remote(yown, ysib, ybs, ybr, sibling)
    ysib_copy.start()
    sk[c, y, zh] = yown[...].astype(BF16)

    def sy_copy(h, k):
        r = ypeer(k)
        return remote(sk.at[c, y, h], sk.at[c, y, h], sys_.at[h, r], syr.at[h, y],
                      device(x, r, z, c))

    def sy_wait(h, k):
        r = ypeer(k)
        remote(sk.at[c, r, h], sk.at[c, r, h], sys_.at[h, r], syr.at[h, r],
               device(x, r, z, c)).wait_recv()

    far_first = (4, 3, 5, 2, 6, 1, 7)
    sz_copy = remote(sk.at[c, y, zh], sk.at[c, y, zh], szs, szr, partner)
    sz_copy.start()
    for k in far_first:
        sy_copy(zh, k).start()

    ysib_copy.wait_recv()
    first = jnp.where(c == 0, yown[...], ysib[...])
    second = jnp.where(c == 0, ysib[...], yown[...])
    both = jnp.concatenate([first, second], axis=1).astype(BF16).astype(F32)
    prod = lax.dot_general(yown[...], both, (((0,), (0,)), ((), ())),
                           precision=HIGHEST, preferred_element_type=F32)
    for h in range(2):
        pm[:, 4 * h:4 * h + 4] = prod[:, h * HALF:(h + 1) * HALF].reshape(NX, 4, 8, HALF)

    def px_copy(k):
        r = xpeer(k)
        return remote(pm.at[r], pxr.at[x], pxs.at[r], pxq.at[x], device(r, y, z, c))

    for k in (2, 1, 3):
        px_copy(k).start()
    pxr[x] = pm[x]

    remote(sk.at[c, y, 1 - zh], sk.at[c, y, 1 - zh], szs, szr, partner).wait_recv()
    for k in far_first:
        sy_copy(1 - zh, k).start()

    for k in range(1, NX):
        r = xpeer(k)
        remote(pm.at[r], pxr.at[r], pxs.at[r], pxq.at[r], device(r, y, z, c)).wait_recv()
    px[...] = (pxr[0] + pxr[1]) + (pxr[2] + pxr[3])

    def pz_copy(k):
        r = zpeer(k)
        return remote(px.at[r], pzr.at[z], pzs.at[r], pzq.at[z], device(x, y, r, c))

    for k in far_first:
        pz_copy(k).start()
    pzr[z] = px[z]
    for k in range(1, NZ):
        r = zpeer(k)
        remote(px.at[r], pzr.at[r], pzs.at[r], pzq.at[r], device(x, y, r, c)).wait_recv()
    pyr[y] = jnp.sum(pzr[...], axis=0)

    def py_copy(k):
        r = ypeer(k)
        return remote(pyr.at[y], pyr.at[y], pys.at[r], pyq.at[y], device(x, r, z, c))

    for k in far_first:
        py_copy(k).start()

    def sb_copy(h):
        return remote(sk.at[c, :, h], sk.at[c, :, h], sbs.at[h], sbr.at[h], sibling)

    for k in range(1, NY):
        sy_wait(zh, k)
    sb_copy(zh).start()

    for k in range(1, NY):
        r = ypeer(k)
        remote(pyr.at[r], pyr.at[r], pys.at[r], pyq.at[r], device(x, r, z, c)).wait_recv()
    cm[c, x, z] = jnp.sum(pyr[...], axis=0)

    def pa_copy(k):
        r = zpeer(k)
        return remote(cm.at[c, x, z], cm.at[c, x, z], pas.at[r], paq.at[z], device(x, y, r, c))

    for k in far_first:
        pa_copy(k).start()

    for k in range(1, NY):
        sy_wait(1 - zh, k)
    sb_copy(1 - zh).start()

    def product(h):
        skt[...] = sk[h].reshape(NY * rows, HALF).T

        def tile(j, carry):
            at = pl.ds(pl.multiple_of(j * 512, 512), 512)
            res = jnp.dot(skt[...], dv[:, at], preferred_element_type=F32)
            res = res.reshape(2, NX, BLOCK, 512)
            cv[pl.ds(2 * h, 2), :, :, at] = res
            cvb[pl.ds(2 * h, 2), :, :, at] = res.astype(BF16)
            return carry

        lax.fori_loop(0, nvar // 512, tile, 0)

    def cx_copy(w, k):
        r = xpeer(k)
        return remote(cvb.at[w, r], cxr.at[w, x], cxs.at[w, r], cxq.at[w, x], device(r, y, z, c))

    product(c)
    for a in range(2):
        for k in (2, 1, 3):
            cx_copy(2 * c + a, k).start()

    for k in range(1, NZ):
        r = zpeer(k)
        remote(cm.at[c, x, r], cm.at[c, x, r], pas.at[r], paq.at[r], device(x, y, r, c)).wait_recv()

    def pb_copy(k):
        r = xpeer(k)
        return remote(cm.at[c, x], cm.at[c, x], pbs.at[r], pbq.at[x], device(r, y, z, c))

    for k in (2, 1, 3):
        pb_copy(k).start()

    for h in range(2):
        remote(sk.at[o, :, h], sk.at[o, :, h], sbs.at[h], sbr.at[h], sibling).wait_recv()
    product(o)
    for a in range(2):
        for k in (2, 1, 3):
            cx_copy(2 * o + a, k).start()

    for k in range(1, NX):
        r = xpeer(k)
        remote(cm.at[c, r], cm.at[c, r], pbs.at[r], pbq.at[r], device(r, y, z, c)).wait_recv()
    pc_copy = remote(cm.at[c], cm.at[c], pcs, pcq, sibling)
    pc_copy.start()
    remote(cm.at[o], cm.at[o], pcs, pcq, sibling).wait_recv()
    left = cm[:, :, 0:4].reshape(K, HALF)
    right = cm[:, :, 4:8].reshape(K, HALF)
    core = jnp.concatenate([left, right], axis=1) * (1.0 / (NX * NZL * NY * rows))
    am[...] = (core + core.T) * 0.5

    def cz_copy(w):
        return remote(czs.at[w], czr.at[zl], czs_s.at[w], czq.at[zl],
                      device(x, y, zh * NZL + w, c))

    lane_at = lax.broadcasted_iota(jnp.int32, (SLAB, K), 1)
    sub_at = lax.broadcasted_iota(jnp.int32, (SLAB, K), 0)

    def slab_step(j, carry):
        start = pl.multiple_of(j * SLAB, SLAB)
        slab = pltpu.roll(am[pl.ds(start, SLAB), :], lax.rem(K - start, K), axis=1)
        u = pltpu.roll(factor_slab(slab, SLAB, K), start, axis=1)
        u = jnp.where(lane_at >= sub_at + start, u, 0.0)
        um[pl.ds(start, SLAB), :] = u
        am[...] -= lax.dot_general(u, u, (((0,), (0,)), ((), ())),
                                   precision=HIGHEST, preferred_element_type=F32)

        w = lax.rem(2 * c + j, NZL)
        for k in range(1, NX):
            r = xpeer(k)
            remote(cvb.at[w, r], cxr.at[w, r], cxs.at[w, r], cxq.at[w, r],
                   device(r, y, z, c)).wait_recv()
        acc = cv[w, x]
        for k in range(1, NX):
            acc = acc + cxr[w, xpeer(k)].astype(F32)

        @pl.when(w == zl)
        def _():
            zacc[...] = acc

        @pl.when(w != zl)
        def _():
            czs[w] = acc.astype(BF16)
            cz_copy(w).start()

        return carry

    lax.fori_loop(0, K // SLAB, slab_step, 0)
    lm[...] = um[...].T
    factor_copy = pltpu.make_async_copy(lm, factor_out, outs.at[0])
    factor_copy.start()

    acc = zacc[...]
    for k in range(1, NZL):
        r = lax.rem(zl + k, NZL)
        remote(czs.at[r], czr.at[r], czs_s.at[r], czq.at[r],
               device(x, y, zh * NZL + r, c)).wait_recv()
        acc = acc + czr[r].astype(F32)
    covv[...] = acc * (1.0 / math.sqrt(NX * NZL * NY * rows))
    cov_copy = pltpu.make_async_copy(covv, cov_out, outs.at[1])
    cov_copy.start()

    def sib_done(r, carry):
        sib_copy(r).wait_send()
        return carry

    lax.fori_loop(0, NY, sib_done, 0)
    for k in range(1, NY):
        y_copy(ypeer(k)).wait_send()
        sy_copy(zh, k).wait_send()
        sy_copy(1 - zh, k).wait_send()
        py_copy(k).wait_send()
        pz_copy(k).wait_send()
        pa_copy(k).wait_send()
    z_copy.wait_send()
    ysib_copy.wait_send()
    sz_copy.wait_send()
    for h in range(2):
        sb_copy(h).wait_send()
    for k in range(1, NX):
        px_copy(k).wait_send()
        pb_copy(k).wait_send()
        for w in range(NZL):
            cx_copy(w, k).wait_send()
    pc_copy.wait_send()
    for k in range(1, NZL):
        cz_copy(lax.rem(zl + k, NZL)).wait_send()
    factor_copy.wait()
    cov_copy.wait()


def per_device(data, test_matrix):
    rows_all, nvar = data.shape
    rows = rows_all // NY
    vm = pltpu.VMEM
    dma = pltpu.SemaphoreType.DMA
    scratch = [
        vm((rows_all, nvar), BF16), vm((nvar, K), BF16),
        vm((2, NY, rows, HALF), F32), vm((NY, rows, HALF), F32), vm((NY, rows, HALF), F32),
        vm((NY, rows, HALF), F32),
        vm((rows // 2, HALF), F32), vm((rows // 2, HALF), F32),
        vm((rows // 2, HALF), F32), vm((rows // 2, HALF), F32),
        vm((2, NY, 2, rows // 2, HALF), BF16), vm((HALF, rows_all), BF16),
        vm((NX, NZ, 8, HALF), F32), vm((NX, NZ, 8, HALF), F32), vm((NZ, 8, HALF), F32),
        vm((NZ, 8, HALF), F32), vm((NY, 8, HALF), F32), vm((2, NX, NZ, 8, HALF), F32),
        vm((K, K), F32), vm((K, K), F32), vm((K, K), F32),
        vm((NZL, NX, BLOCK, nvar), F32), vm((NZL, NX, BLOCK, nvar), BF16),
        vm((NZL, NX, BLOCK, nvar), BF16), vm((NZL, BLOCK, nvar), BF16),
        vm((NZL, BLOCK, nvar), BF16), vm((BLOCK, nvar), F32), vm((BLOCK, nvar), F32),
        dma((NY + 1,)), dma((NY,)), dma((NY,)), dma((NY,)), dma((NY,)),
        dma, dma, dma, dma, dma((2, NY)), dma((2, NY)), dma((2,)), dma((2,)), dma, dma,
        dma((NX,)), dma((NX,)), dma((NZ,)), dma((NZ,)), dma((NY,)), dma((NY,)),
        dma((NZ,)), dma((NZ,)), dma((NX,)), dma((NX,)), dma, dma,
        dma((NZL, NX)), dma((NZL, NX)), dma((NZL,)), dma((NZL,)), dma((2,)),
    ]
    any_ = pl.BlockSpec(memory_space=pl.ANY)
    cov_t, factor = pl.pallas_call(
        kernel,
        out_shape=(jax.ShapeDtypeStruct((BLOCK, nvar), F32), jax.ShapeDtypeStruct((K, K), F32)),
        in_specs=[any_, any_],
        out_specs=(any_, any_),
        scratch_shapes=scratch,
        compiler_params=pltpu.CompilerParams(
            collective_id=0, has_side_effects=True, vmem_limit_bytes=48 * 1024 * 1024
        ),
        cost_estimate=pl.CostEstimate(
            flops=4 * rows_all * nvar * K, bytes_accessed=2 * nvar * (rows_all + K),
            transcendentals=0,
        ),
        name="sketch",
    )(data, test_matrix)
    return (cov_t.T, factor)


def solution(mesh):
    return jax.shard_map(
        per_device,
        mesh=mesh,
        in_specs=(P("sample", "var"), P("var", None)),
        out_specs=(P("var", "sample"), P()),
        check_vma=False,
    )
```

time: 773 us -> 79.7 us (0.10)
  waiting for transfers between devices: 521 us -> 0 us
  blocking collectives: 181 us -> 0 us
  Pallas kernels: 0 us -> 74.4 us
  other arithmetic: 36.8 us -> 0 us
  between operations: 15.4 us -> 0.65 us
  matrix products: 11.2 us -> 0 us
    psum x2 -> x0, waiting for transfers between devices: 521 us -> none  [the longest x1 348 us: per_device(): core = lax.psum(core_term, 'var')]
    psum x1 -> x0, blocking collectives: 181 us -> none  [per_device(): sketch = lax.psum(term, 'var').astype(jnp.bfloat16)]
    pallas_call x0 -> x1, Pallas kernels: none -> 74.4 us  [per_device(): pl.pallas_call(kernel, out_shape=(jax.ShapeDtypeStruct((BLOCK, nvar), F32...]
    another operation x6 -> x0, other arithmetic: 34 us -> none  [per_device(): core_factor = jnp.linalg.cholesky(core)]
    dot_general x3 -> x0, matrix products: 9.02 us -> none  [the longest x1 3.64 us: precise_product(): lax.dot_general(left, right, (((0,), (0,)), ((), ())), precision=lax.Prec...]
  transfers between devices with their start and end apart: 2 -> 0, of which waited for: 2 -> 0; matrix products, arithmetic and copies ran while one was open for 0% -> 0% of each run, Pallas kernels for 0% -> 0%
where the time goes in v1:
time: 79.7 us; the launch traced here: 79.5 us
  Pallas kernels  74.4 us (93%)
  local copies, waits for them, and re-layouts  4.47 us (6%)
    pallas_call x1, Pallas kernels, per_device(): pl.pallas_call(kernel, out_shape=(jax.ShapeDtypeStruct((BLOCK, nvar), F32...  74.4 us
    unnamed x6, local copies, waits for them, and re-layouts  4.47 us

profile of v1, /device:TPU:1, one launch (start us, length us, event | category | flops | bytes accessed | tf_op | source)
XLA Modules:
  0.0 79.5 jit_solution(4045580076875439436)
XLA Ops:
  0.6 0.0 copy-start
  0.6 1.9 %copy-done = bf16[768,2048]{1,0:T(8,128)(2,1)S(1)} copy-done((bf16[768,2048]{1,0:T(8,128)(2,1)S(1)}, bf16[768,2048]{1,0:T(8,128)(2,1)}, u32[]{:S(2)}) %copy-start) | copy-done | bytes 3145752
  2.5 0.0 copy-start.1
  2.5 1.2 %copy-done.1 = bf16[2048,256]{1,0:T(8,128)(2,1)S(1)} copy-done((bf16[2048,256]{1,0:T(8,128)(2,1)S(1)}, bf16[2048,256]{1,0:T(8,128)(2,1)}, u32[]{:S(2)}) %copy-start.1) | copy-done | bytes 1048600
  3.7 74.4 %sketch.1 = (f32[16,2048]{1,0:T(8,128)S(1)}, f32[256,256]{1,0:T(8,128)S(1)}) custom-call(bf16[768,2048]{1,0:T(8,128)(2,1)S(1)} %copy-done, bf16[2048,256]{1,0:T(8,128)(2,1)S(1)} %copy-done.1), custom_call_target="tpu_custom_call" | custom-call | flops 1610612736 | bytes 4194304 | tf_op jit(solution)/shard_map/sketch/pallas_call | solution.py:433
  78.1 0.7 copy.6
  78.8 0.7 copy.7
Async XLA Ops:
  0.6 1.9 %copy-start = (bf16[768,2048]{1,0:T(8,128)(2,1)S(1)}, bf16[768,2048]{1,0:T(8,128)(2,1)}, u32[]{:S(2)}) copy-start(bf16[768,2048]{1,0:T(8,128)(2,1)} %data.1) | copy-start | bytes 9437188
  2.5 1.2 %copy-start.1 = (bf16[2048,256]{1,0:T(8,128)(2,1)S(1)}, bf16[2048,256]{1,0:T(8,128)(2,1)}, u32[]{:S(2)}) copy-start(bf16[2048,256]{1,0:T(8,128)(2,1)} %test.1) | copy-start | bytes 3145732

commit v2 on v1

v2 whole, which is shorter than its diff:
```python
import math

import jax
import jax.numpy as jnp
from jax import lax
from jax.experimental import pallas as pl
from jax.experimental.pallas import tpu as pltpu
from jax.sharding import PartitionSpec as P

MESH = pl.DeviceIdType.MESH
HIGHEST = lax.Precision.HIGHEST
F32 = jnp.float32
BF16 = jnp.bfloat16

NX, NY, NZ = 4, 8, 8
NZL = 4
K = 256
HALF = 128
BLOCK = 16
SLAB = 64


def position():
    s = lax.axis_index("sample")
    v = lax.axis_index("var")
    x = lax.rem(s, NX)
    zl = s // NX
    c = lax.rem(v, 2)
    zh = lax.rem(v // 2, 2)
    y = v // 4
    return x, y, zh * NZL + zl, c


def device(x, y, z, c):
    return (lax.rem(z, NZL) * NX + x, y * 4 + (z // NZL) * 2 + c)


def remote(src, dst, send, recv, target):
    return pltpu.make_async_remote_copy(
        src_ref=src, dst_ref=dst, send_sem=send, recv_sem=recv,
        device_id=target, device_id_type=MESH,
    )


def factor_slab(block, rows, lanes):
    wide = lanes // HALF

    def spread(a):
        return jnp.concatenate([a] * wide, axis=1)

    count = rows // 8
    tiles = [block[8 * t:8 * t + 8, :] for t in range(count)]
    done = []
    row_at = lax.broadcasted_iota(jnp.int32, (8, lanes), 0)
    for t in range(count):
        tile = tiles[t]
        base = 8 * t
        below = range(t + 1, count)
        piv = {}
        for i in range(8):
            for j in range(i + 1):
                piv[i, j] = jnp.broadcast_to(tile[i:i + 1, base + j:base + j + 1], (8, HALF))
        cols = {}
        for u in below:
            for k in range(8):
                cols[u, k] = jnp.broadcast_to(tiles[u][:, base + k:base + k + 1], (8, HALF))
        rowv = [jnp.broadcast_to(tile[i:i + 1, :], (8, lanes)) for i in range(8)]
        for k in range(8):
            inv = lax.rsqrt(piv[k, k])
            rowv[k] = rowv[k] * spread(inv)
            for i in range(k + 1, 8):
                piv[i, k] = piv[i, k] * inv
            for u in below:
                cols[u, k] = cols[u, k] * inv
            for i in range(k + 1, 8):
                for j in range(k + 1, i + 1):
                    piv[i, j] = piv[i, j] - piv[i, k] * piv[j, k]
                rowv[i] = rowv[i] - spread(piv[i, k]) * rowv[k]
                for u in below:
                    cols[u, i] = cols[u, i] - piv[i, k] * cols[u, k]
            for u in below:
                tiles[u] = tiles[u] - spread(cols[u, k]) * rowv[k]
        out = rowv[7]
        for i in range(7):
            out = jnp.where(row_at == i, rowv[i], out)
        done.append(out)
    return jnp.concatenate(done, axis=0)


def kernel(data, test, cov_out, factor_out,
           dv, tv, part, sib, q, yrecv, zrecv, ysum, sk, pxr, pzr, cm, am, um, lm,
           cv, cvb, cxr, czs, czr, zacc, covv,
           ld, xs, xr, ys, yr, zs, zr, sys_, syr, sbs, sbr,
           pxs, pxq, pzs, pzq, pys, pyq, pcs, pcq, cxs, cxq, czs_s, czq, outs):
    x, y, z, c = position()
    zl = lax.rem(z, NZL)
    zh = z // NZL
    o = 1 - c
    nrow, nvar = data.shape
    part_rows = nrow // 2
    sibling = device(x, y, z, o)
    partner = device(x, y, lax.rem(z + NZL, NZ), c)
    far_first = (4, 3, 5, 2, 6, 1, 7)

    def ypeer(k):
        return lax.rem(y + k, NY)

    def zpeer(k):
        return lax.rem(zl + k, NZL)

    def zdev(w):
        return device(x, y, zh * NZL + w, c)

    def xpeer(k):
        return lax.rem(x + k, NX)

    tcopy = pltpu.make_async_copy(test, tv, ld.at[2])
    tcopy.start()

    def dcopy(i):
        at = pl.ds(i * part_rows, part_rows)
        return pltpu.make_async_copy(data.at[at, :], dv.at[at, :], ld.at[i])

    for i in range(2):
        dcopy(i).start()

    barrier = pltpu.get_barrier_semaphore()
    peers = [sibling, partner]
    peers += [device(x, ypeer(k), z, c) for k in range(1, NY)]
    peers += [zdev(zpeer(k)) for k in range(1, NZL)]
    peers += [device(xpeer(k), y, z, c) for k in range(1, NX)]
    for p in peers:
        pl.semaphore_signal(barrier, inc=1, device_id=p, device_id_type=MESH)

    def sib_copy(i):
        at = pl.ds(i * part_rows, part_rows)
        return remote(part.at[o, :, at], sib.at[:, at], xs.at[i], xr.at[i], sibling)

    def y_copy(r):
        return remote(q.at[r], yrecv.at[y], ys.at[r], yr.at[y], device(x, r, z, c))

    tcopy.wait()
    for i in range(2):
        dcopy(i).wait()
        at = slice(i * part_rows, (i + 1) * part_rows)
        p = jnp.dot(dv[at, :], tv[...], preferred_element_type=F32).T
        part[0, :, at] = p[:HALF]
        part[1, :, at] = p[HALF:]
        if i == 0:
            pl.semaphore_wait(barrier, len(peers))
        sib_copy(i).start()
    for i in range(2):
        sib_copy(i).wait_recv()
        at = slice(i * part_rows, (i + 1) * part_rows)
        q[:, :, at] = (part[c, :, at] + sib[:, at]).reshape(NY, BLOCK, part_rows)
    for k in far_first:
        y_copy(ypeer(k)).start()

    total = q[y]
    for k in range(1, NY):
        r = ypeer(k)
        remote(q.at[r], yrecv.at[r], ys.at[r], yr.at[r], device(x, r, z, c)).wait_recv()
        total = total + yrecv[r]
    q[y] = total
    z_copy = remote(q.at[y], zrecv, zs, zr, partner)
    z_copy.start()
    z_copy.wait_recv()
    ysum[...] = (total + zrecv[...]) * (1.0 / K)
    sk[c, y] = ysum[...].astype(BF16)

    def sy_copy(k):
        r = ypeer(k)
        return remote(sk.at[c, y], sk.at[c, y], sys_.at[r], syr.at[y], device(x, r, z, c))

    for k in far_first:
        sy_copy(k).start()
    for k in range(1, NY):
        r = ypeer(k)
        remote(sk.at[c, r], sk.at[c, r], sys_.at[r], syr.at[r], device(x, r, z, c)).wait_recv()
    sb_copy = remote(sk.at[c], sk.at[c], sbs, sbr, sibling)
    sb_copy.start()

    def product(h):
        left = sk[h].reshape(HALF, nrow)

        def tile(j, carry):
            at = pl.ds(pl.multiple_of(j * 1024, 1024), 1024)
            res = jnp.dot(left, dv[:, at], preferred_element_type=F32)
            res = res.reshape(2, NX, BLOCK, 1024)
            cv[pl.ds(2 * h, 2), :, :, at] = res
            cvb[pl.ds(2 * h, 2), :, :, at] = res.astype(BF16)
            return carry

        lax.fori_loop(0, nvar // 1024, tile, 0)

    def cx_copy(w, k):
        r = xpeer(k)
        return remote(cvb.at[w, r], cxr.at[w, x], cxs.at[w, r], cxq.at[w, x], device(r, y, z, c))

    def cz_copy(w):
        return remote(czs.at[w], czr.at[zl], czs_s.at[w], czq.at[zl], zdev(w))

    def x_sum(w):
        for k in range(1, NX):
            r = xpeer(k)
            remote(cvb.at[w, r], cxr.at[w, r], cxs.at[w, r], cxq.at[w, r],
                   device(r, y, z, c)).wait_recv()
        acc = cv[w, x]
        for k in range(1, NX):
            acc = acc + cxr[w, xpeer(k)].astype(F32)

        @pl.when(w == zl)
        def _():
            zacc[...] = acc

        @pl.when(w != zl)
        def _():
            czs[w] = acc.astype(BF16)
            cz_copy(w).start()

    product(c)
    remote(sk.at[o], sk.at[o], sbs, sbr, sibling).wait_recv()

    y1 = ysum[...].astype(BF16)
    rest = ysum[...] - y1.astype(F32)
    y2 = rest.astype(BF16)
    y3 = (rest - y2.astype(F32)).astype(BF16)
    terms = lax.dot_general(
        jnp.concatenate([y1, y2, y3], axis=0), sk[...].reshape(K, nrow),
        (((1,), (1,)), ((), ())), preferred_element_type=F32,
    )
    terms = (terms[2 * BLOCK:] + terms[BLOCK:2 * BLOCK]) + terms[:BLOCK]
    pxr[x] = terms * (1.0 / (NX * NZL * nrow))

    def px_copy(k):
        r = xpeer(k)
        return remote(pxr.at[x], pxr.at[x], pxs.at[r], pxq.at[x], device(r, y, z, c))

    for k in (2, 1, 3):
        px_copy(k).start()
    for a in range(2):
        for k in (2, 1, 3):
            cx_copy(2 * c + a, k).start()
    product(o)
    for a in range(2):
        for k in (2, 1, 3):
            cx_copy(2 * o + a, k).start()

    for k in range(1, NX):
        r = xpeer(k)
        remote(pxr.at[r], pxr.at[r], pxs.at[r], pxq.at[r], device(r, y, z, c)).wait_recv()
    pzr[zl] = (pxr[0] + pxr[1]) + (pxr[2] + pxr[3])

    def pz_copy(k):
        r = zpeer(k)
        return remote(pzr.at[zl], pzr.at[zl], pzs.at[r], pzq.at[zl], zdev(r))

    for k in (3, 2, 1):
        pz_copy(k).start()
    x_sum(2 * c)
    for k in range(1, NZL):
        r = zpeer(k)
        remote(pzr.at[r], pzr.at[r], pzs.at[r], pzq.at[r], zdev(r)).wait_recv()
    cm[c, y] = (pzr[0] + pzr[1]) + (pzr[2] + pzr[3])

    def py_copy(k):
        r = ypeer(k)
        return remote(cm.at[c, y], cm.at[c, y], pys.at[r], pyq.at[y], device(x, r, z, c))

    for k in far_first:
        py_copy(k).start()
    x_sum(2 * c + 1)
    for k in range(1, NY):
        r = ypeer(k)
        remote(cm.at[c, r], cm.at[c, r], pys.at[r], pyq.at[r], device(x, r, z, c)).wait_recv()
    pc_copy = remote(cm.at[c], cm.at[c], pcs, pcq, sibling)
    pc_copy.start()
    remote(cm.at[o], cm.at[o], pcs, pcq, sibling).wait_recv()
    core = cm[...].reshape(K, K)
    am[...] = (core + core.T) * 0.5

    lane_at = lax.broadcasted_iota(jnp.int32, (SLAB, K), 1)
    sub_at = lax.broadcasted_iota(jnp.int32, (SLAB, K), 0)

    def slab_step(j, carry):
        start = pl.multiple_of(j * SLAB, SLAB)
        slab = pltpu.roll(am[pl.ds(start, SLAB), :], lax.rem(K - start, K), axis=1)
        u = pltpu.roll(factor_slab(slab, SLAB, K), start, axis=1)
        u = jnp.where(lane_at >= sub_at + start, u, 0.0)
        um[pl.ds(start, SLAB), :] = u
        am[...] -= lax.dot_general(u, u, (((0,), (0,)), ((), ())),
                                   precision=HIGHEST, preferred_element_type=F32)

        @pl.when(j < 2)
        def _():
            x_sum(2 * o + j)

        return carry

    lax.fori_loop(0, K // SLAB, slab_step, 0)
    lm[...] = um[...].T
    factor_copy = pltpu.make_async_copy(lm, factor_out, outs.at[0])
    factor_copy.start()

    acc = zacc[...]
    for k in range(1, NZL):
        r = zpeer(k)
        remote(czs.at[r], czr.at[r], czs_s.at[r], czq.at[r], zdev(r)).wait_recv()
        acc = acc + czr[r].astype(F32)
    covv[...] = acc * (1.0 / math.sqrt(NX * NZL * nrow))
    cov_copy = pltpu.make_async_copy(covv, cov_out, outs.at[1])
    cov_copy.start()

    for i in range(2):
        sib_copy(i).wait_send()
    for k in range(1, NY):
        y_copy(ypeer(k)).wait_send()
        sy_copy(k).wait_send()
        py_copy(k).wait_send()
    z_copy.wait_send()
    sb_copy.wait_send()
    for k in range(1, NX):
        px_copy(k).wait_send()
        for w in range(NZL):
            cx_copy(w, k).wait_send()
    pc_copy.wait_send()
    for k in range(1, NZL):
        pz_copy(k).wait_send()
        cz_copy(zpeer(k)).wait_send()
    factor_copy.wait()
    cov_copy.wait()


def per_device(data, test_matrix):
    rows_all, nvar = data.shape
    vm = pltpu.VMEM
    dma = pltpu.SemaphoreType.DMA
    scratch = [
        vm((rows_all, nvar), BF16), vm((nvar, K), BF16),
        vm((2, HALF, rows_all), F32), vm((HALF, rows_all), F32),
        vm((NY, BLOCK, rows_all), F32), vm((NY, BLOCK, rows_all), F32),
        vm((BLOCK, rows_all), F32), vm((BLOCK, rows_all), F32),
        vm((2, NY, BLOCK, rows_all), BF16),
        vm((NX, BLOCK, K), F32), vm((NZL, BLOCK, K), F32), vm((2, NY, BLOCK, K), F32),
        vm((K, K), F32), vm((K, K), F32), vm((K, K), F32),
        vm((NZL, NX, BLOCK, nvar), F32), vm((NZL, NX, BLOCK, nvar), BF16),
        vm((NZL, NX, BLOCK, nvar), BF16), vm((NZL, BLOCK, nvar), BF16),
        vm((NZL, BLOCK, nvar), BF16), vm((BLOCK, nvar), F32), vm((BLOCK, nvar), F32),
        dma((3,)), dma((2,)), dma((2,)), dma((NY,)), dma((NY,)),
        dma, dma, dma((NY,)), dma((NY,)), dma, dma,
        dma((NX,)), dma((NX,)), dma((NZL,)), dma((NZL,)), dma((NY,)), dma((NY,)),
        dma, dma, dma((NZL, NX)), dma((NZL, NX)), dma((NZL,)), dma((NZL,)), dma((2,)),
    ]
    any_ = pl.BlockSpec(memory_space=pl.ANY)
    cov_t, factor = pl.pallas_call(
        kernel,
        out_shape=(jax.ShapeDtypeStruct((BLOCK, nvar), F32), jax.ShapeDtypeStruct((K, K), F32)),
        in_specs=[any_, any_],
        out_specs=(any_, any_),
        scratch_shapes=scratch,
        compiler_params=pltpu.CompilerParams(
            collective_id=0, has_side_effects=True, vmem_limit_bytes=62 * 1024 * 1024
        ),
        cost_estimate=pl.CostEstimate(
            flops=4 * rows_all * nvar * K, bytes_accessed=2 * nvar * (rows_all + K),
            transcendentals=0,
        ),
        name="sketch",
    )(data, test_matrix)
    return (cov_t.T, factor)


def solution(mesh):
    return jax.shard_map(
        per_device,
        mesh=mesh,
        in_specs=(P("sample", "var"), P("var", None)),
        out_specs=(P("var", "sample"), P()),
        check_vma=False,
    )
```

time: 79.7 us -> 72.2 us (0.906)
  Pallas kernels: 74.4 us -> 68.1 us
  local copies, waits for them, and re-layouts: 4.47 us -> 3.24 us
    pallas_call x1, Pallas kernels: 74.4 us -> 68.1 us  [per_device(): pl.pallas_call(kernel, out_shape=(jax.ShapeDtypeStruct((BLOCK, nvar), F32...]
    unnamed x6 -> x2, local copies, waits for them, and re-layouts: 4.47 us -> 3.24 us
where the time goes in v2:
time: 72.2 us; the launch traced here: 72 us
  Pallas kernels  68.1 us (94%)
  local copies, waits for them, and re-layouts  3.24 us (4%)
    pallas_call x1, Pallas kernels, per_device(): pl.pallas_call(kernel, out_shape=(jax.ShapeDtypeStruct((BLOCK, nvar), F32...  68.1 us
    unnamed x2, local copies, waits for them, and re-layouts  3.24 us

profile of v2, /device:TPU:1, one launch (start us, length us, event | category | flops | bytes accessed | tf_op | source)
XLA Modules:
  0.0 72.0 jit_solution(7457866699991280290)
XLA Ops:
  0.6 68.1 %sketch.1 = (f32[16,2048]{1,0:T(8,128)}, f32[256,256]{1,0:T(8,128)}) custom-call(bf16[768,2048]{1,0:T(8,128)(2,1)} %data.1, bf16[2048,256]{1,0:T(8,128)(2,1)} %test.1), custom_call_target="tpu_custom_call" | custom-call | flops 1610612736 | bytes 4194304 | tf_op jit(solution)/shard_map/sketch/pallas_call | solution.py:355
  68.8 1.6 %copy.6 = f32[2048,16]{0,1:T(8,128)} copy(f32[2048,16]{0,1:T(8,128)} %bitcast.1) | data formatting | bytes 262144
  70.3 1.7 %copy.7 = f32[256,256]{1,0:T(8,128)} copy(f32[256,256]{1,0:T(8,128)} %get-tuple-element.9) | data formatting | bytes 524288

commit v3 on v2

--- a/solution.py
+++ b/solution.py
@@ -18,6 +18,8 @@
 HALF = 128
 BLOCK = 16
 SLAB = 64
+SPAN = 83.0
+TINY = 1e-30
 
 
 def position():
@@ -40,6 +42,19 @@
         src_ref=src, dst_ref=dst, send_sem=send, recv_sem=recv,
         device_id=target, device_id_type=MESH,
     )
+
+
+def encode(a):
+    top = jnp.maximum(jnp.max(jnp.abs(a), axis=1, keepdims=True), TINY) * 1.01
+    scale = jnp.broadcast_to(top, (a.shape[0], HALF)).astype(BF16)
+    wide = jnp.concatenate([SPAN / scale.astype(F32)] * (a.shape[1] // HALF), axis=1)
+    return jnp.concatenate([jnp.exp(a * wide).astype(BF16), scale], axis=1)
+
+
+def decode(e):
+    lanes = e.shape[1] - HALF
+    scale = e[:, lanes:].astype(F32) * (1.0 / SPAN)
+    return jnp.log(e[:, :lanes].astype(F32)) * jnp.concatenate([scale] * (lanes // HALF), axis=1)
 
 
 def factor_slab(block, rows, lanes):
@@ -88,10 +103,10 @@
 
 
 def kernel(data, test, cov_out, factor_out,
-           dv, tv, part, sib, q, yrecv, zrecv, ysum, sk, pxr, pzr, cm, am, um, lm,
-           cv, cvb, cxr, czs, czr, zacc, covv,
+           dv, tv, part, sib, q, yrecv, zrecv, ysum, sk, pxr, pzr, cm, am, um,
+           cv, cvb, cxr, czs, czr, zacc,
            ld, xs, xr, ys, yr, zs, zr, sys_, syr, sbs, sbr,
-           pxs, pxq, pzs, pzq, pys, pyq, pcs, pcq, cxs, cxq, czs_s, czq, outs):
+           pxs, pxq, pzs, pzq, pys, pyq, pcs, pcq, cxs, cxq, czs_s, czq):
     x, y, z, c = position()
     zl = lax.rem(z, NZL)
     zh = z // NZL
@@ -152,20 +167,22 @@
     for i in range(2):
         sib_copy(i).wait_recv()
         at = slice(i * part_rows, (i + 1) * part_rows)
-        q[:, :, at] = (part[c, :, at] + sib[:, at]).reshape(NY, BLOCK, part_rows)
+        part[c, :, at] = part[c, :, at] + sib[:, at]
     for k in far_first:
-        y_copy(ypeer(k)).start()
-
-    total = q[y]
+        r = ypeer(k)
+        q[r] = encode(part[c, pl.ds(pl.multiple_of(r * BLOCK, BLOCK), BLOCK), :])
+        y_copy(r).start()
+
+    total = part[c, pl.ds(pl.multiple_of(y * BLOCK, BLOCK), BLOCK), :]
     for k in range(1, NY):
         r = ypeer(k)
         remote(q.at[r], yrecv.at[r], ys.at[r], yr.at[r], device(x, r, z, c)).wait_recv()
-        total = total + yrecv[r]
-    q[y] = total
+        total = total + decode(yrecv[r])
+    q[y] = encode(total)
     z_copy = remote(q.at[y], zrecv, zs, zr, partner)
     z_copy.start()
     z_copy.wait_recv()
-    ysum[...] = (total + zrecv[...]) * (1.0 / K)
+    ysum[...] = (decode(q[y]) + decode(zrecv[...])) * (1.0 / K)
     sk[c, y] = ysum[...].astype(BF16)
 
     def sy_copy(k):
@@ -288,8 +305,11 @@
         u = pltpu.roll(factor_slab(slab, SLAB, K), start, axis=1)
         u = jnp.where(lane_at >= sub_at + start, u, 0.0)
         um[pl.ds(start, SLAB), :] = u
-        am[...] -= lax.dot_general(u, u, (((0,), (0,)), ((), ())),
-                                   precision=HIGHEST, preferred_element_type=F32)
+
+        @pl.when(j < K // SLAB - 1)
+        def _():
+            am[...] -= lax.dot_general(u, u, (((0,), (0,)), ((), ())),
+                                       precision=HIGHEST, preferred_element_type=F32)
 
         @pl.when(j < 2)
         def _():
@@ -298,18 +318,14 @@
         return carry
 
     lax.fori_loop(0, K // SLAB, slab_step, 0)
-    lm[...] = um[...].T
-    factor_copy = pltpu.make_async_copy(lm, factor_out, outs.at[0])
-    factor_copy.start()
+    factor_out[...] = um[...].T
 
     acc = zacc[...]
     for k in range(1, NZL):
         r = zpeer(k)
         remote(czs.at[r], czr.at[r], czs_s.at[r], czq.at[r], zdev(r)).wait_recv()
         acc = acc + czr[r].astype(F32)
-    covv[...] = acc * (1.0 / math.sqrt(NX * NZL * nrow))
-    cov_copy = pltpu.make_async_copy(covv, cov_out, outs.at[1])
-    cov_copy.start()
+    cov_out[...] = acc * (1.0 / math.sqrt(NX * NZL * nrow))
 
     for i in range(2):
         sib_copy(i).wait_send()
@@ -327,8 +343,6 @@
     for k in range(1, NZL):
         pz_copy(k).wait_send()
         cz_copy(zpeer(k)).wait_send()
-    factor_copy.wait()
-    cov_copy.wait()
 
 
 def per_device(data, test_matrix):
@@ -338,25 +352,26 @@
     scratch = [
         vm((rows_all, nvar), BF16), vm((nvar, K), BF16),
         vm((2, HALF, rows_all), F32), vm((HALF, rows_all), F32),
-        vm((NY, BLOCK, rows_all), F32), vm((NY, BLOCK, rows_all), F32),
-        vm((BLOCK, rows_all), F32), vm((BLOCK, rows_all), F32),
+        vm((NY, BLOCK, rows_all + HALF), BF16), vm((NY, BLOCK, rows_all + HALF), BF16),
+        vm((BLOCK, rows_all + HALF), BF16), vm((BLOCK, rows_all), F32),
         vm((2, NY, BLOCK, rows_all), BF16),
         vm((NX, BLOCK, K), F32), vm((NZL, BLOCK, K), F32), vm((2, NY, BLOCK, K), F32),
-        vm((K, K), F32), vm((K, K), F32), vm((K, K), F32),
+        vm((K, K), F32), vm((K, K), F32),
         vm((NZL, NX, BLOCK, nvar), F32), vm((NZL, NX, BLOCK, nvar), BF16),
         vm((NZL, NX, BLOCK, nvar), BF16), vm((NZL, BLOCK, nvar), BF16),
-        vm((NZL, BLOCK, nvar), BF16), vm((BLOCK, nvar), F32), vm((BLOCK, nvar), F32),
+        vm((NZL, BLOCK, nvar), BF16), vm((BLOCK, nvar), F32),
         dma((3,)), dma((2,)), dma((2,)), dma((NY,)), dma((NY,)),
         dma, dma, dma((NY,)), dma((NY,)), dma, dma,
         dma((NX,)), dma((NX,)), dma((NZL,)), dma((NZL,)), dma((NY,)), dma((NY,)),
-        dma, dma, dma((NZL, NX)), dma((NZL, NX)), dma((NZL,)), dma((NZL,)), dma((2,)),
+        dma, dma, dma((NZL, NX)), dma((NZL, NX)), dma((NZL,)), dma((NZL,)),
     ]
     any_ = pl.BlockSpec(memory_space=pl.ANY)
+    vmem = pl.BlockSpec(memory_space=pltpu.VMEM)
     cov_t, factor = pl.pallas_call(
         kernel,
-        out_shape=(jax.ShapeDtypeStruct((BLOCK, nvar), F32), jax.ShapeDtypeStruct((K, K), F32)),
+        out_shape=(pltpu.VMEM((BLOCK, nvar), F32), pltpu.VMEM((K, K), F32)),
         in_specs=[any_, any_],
-        out_specs=(any_, any_),
+        out_specs=(vmem, vmem),
         scratch_shapes=scratch,
         compiler_params=pltpu.CompilerParams(
             collective_id=0, has_side_effects=True, vmem_limit_bytes=62 * 1024 * 1024

time: 72.2 us -> 65 us (0.900)
  Pallas kernels: 68.1 us -> 62.9 us
  local copies, waits for them, and re-layouts: 3.24 us -> 1.36 us
    pallas_call x1, Pallas kernels: 68.1 us -> 62.9 us  [per_device(): pl.pallas_call(kernel, out_shape=(pltpu.VMEM((BLOCK, nvar), F32), pltpu.V...]
    unnamed x2, local copies, waits for them, and re-layouts: 3.24 us -> 1.36 us
where the time goes in v3:
time: 65 us; the launch traced here: 64.9 us
  Pallas kernels  62.9 us (97%)
  local copies, waits for them, and re-layouts  1.36 us (2%)
    pallas_call x1, Pallas kernels, per_device(): pl.pallas_call(kernel, out_shape=(pltpu.VMEM((BLOCK, nvar), F32), pltpu.V...  62.9 us
    unnamed x2, local copies, waits for them, and re-layouts  1.36 us

profile of v3, /device:TPU:1, one launch (start us, length us, event | category | flops | bytes accessed | tf_op | source)
XLA Modules:
  0.0 64.9 jit_solution(10773345872082156765)
XLA Ops:
  0.6 62.9 %sketch.1 = (f32[16,2048]{1,0:T(8,128)S(1)}, f32[256,256]{1,0:T(8,128)S(1)}) custom-call(bf16[768,2048]{1,0:T(8,128)(2,1)} %data.1, bf16[2048,256]{1,0:T(8,128)(2,1)} %test.1), custom_call_target="tpu_custom_call" | custom-call | flops 1610612736 | bytes 4194304 | tf_op jit(solution)/shard_map/sketch/pallas_call | solution.py:370
  63.5 0.7 %copy.6 = f32[2048,16]{0,1:T(8,128)} copy(f32[2048,16]{0,1:T(8,128)S(1)} %bitcast.1) | data formatting | bytes 262144
  64.2 0.7 %copy.7 = f32[256,256]{1,0:T(8,128)} copy(f32[256,256]{1,0:T(8,128)S(1)} %get-tuple-element.7) | data formatting | bytes 524288

commit v4 on v3

--- a/solution.py
+++ b/solution.py
@@ -57,7 +57,7 @@
     return jnp.log(e[:, :lanes].astype(F32)) * jnp.concatenate([scale] * (lanes // HALF), axis=1)
 
 
-def factor_slab(block, rows, lanes):
+def factor_slab(block, rows, lanes, held):
     wide = lanes // HALF
 
     def spread(a):
@@ -70,31 +70,41 @@
     for t in range(count):
         tile = tiles[t]
         base = 8 * t
-        below = range(t + 1, count)
+        for j in range(8):
+            held[t % 2, j] = jnp.broadcast_to(tile[:, base + j:base + j + 1], (8, HALF))
         piv = {}
         for i in range(8):
             for j in range(i + 1):
-                piv[i, j] = jnp.broadcast_to(tile[i:i + 1, base + j:base + j + 1], (8, HALF))
-        cols = {}
-        for u in below:
-            for k in range(8):
-                cols[u, k] = jnp.broadcast_to(tiles[u][:, base + k:base + k + 1], (8, HALF))
-        rowv = [jnp.broadcast_to(tile[i:i + 1, :], (8, lanes)) for i in range(8)]
-        for k in range(8):
-            inv = lax.rsqrt(piv[k, k])
-            rowv[k] = rowv[k] * spread(inv)
-            for i in range(k + 1, 8):
-                piv[i, k] = piv[i, k] * inv
-            for u in below:
-                cols[u, k] = cols[u, k] * inv
-            for i in range(k + 1, 8):
-                for j in range(k + 1, i + 1):
-                    piv[i, j] = piv[i, j] - piv[i, k] * piv[j, k]
-                rowv[i] = rowv[i] - spread(piv[i, k]) * rowv[k]
-                for u in below:
-                    cols[u, i] = cols[u, i] - piv[i, k] * cols[u, k]
-            for u in below:
-                tiles[u] = tiles[u] - spread(cols[u, k]) * rowv[k]
+                piv[i, j] = jnp.broadcast_to(held[t % 2, j, i:i + 1, :], (8, HALF))
+        inv = {}
+        for k in range(0, 8, 2):
+            first, cross, second = piv[k, k], piv[k + 1, k], piv[k + 1, k + 1]
+            root = lax.rsqrt(first)
+            inv[k] = root
+            inv[k + 1] = lax.rsqrt(first * second - cross * cross) * (first * root)
+            piv[k + 1, k] = cross * root
+            for i in range(k + 2, 8):
+                piv[i, k] = piv[i, k] * root
+                piv[i, k + 1] = (piv[i, k + 1] - piv[i, k] * piv[k + 1, k]) * inv[k + 1]
+            for i in range(k + 2, 8):
+                for j in range(k + 2, i + 1):
+                    piv[i, j] = piv[i, j] - piv[i, k] * piv[j, k] - piv[i, k + 1] * piv[j, k + 1]
+        rowv = []
+        for i in range(8):
+            v = jnp.broadcast_to(tile[i:i + 1, :], (8, lanes))
+            for k in range(i):
+                v = v - spread(piv[i, k]) * rowv[k]
+            rowv.append(v * spread(inv[i]))
+        for u in range(t + 1, count):
+            cols = []
+            acc = tiles[u]
+            for i in range(8):
+                v = jnp.broadcast_to(tiles[u][:, base + i:base + i + 1], (8, HALF))
+                for k in range(i):
+                    v = v - piv[i, k] * cols[k]
+                cols.append(v * inv[i])
+                acc = acc - spread(cols[i]) * rowv[i]
+            tiles[u] = acc
         out = rowv[7]
         for i in range(7):
             out = jnp.where(row_at == i, rowv[i], out)
@@ -103,7 +113,7 @@
 
 
 def kernel(data, test, cov_out, factor_out,
-           dv, tv, part, sib, q, yrecv, zrecv, ysum, sk, pxr, pzr, cm, am, um,
+           dv, tv, part, sib, q, yrecv, zrecv, ysum, sk, pxr, pzr, cm, am, um, held, root,
            cv, cvb, cxr, czs, czr, zacc,
            ld, xs, xr, ys, yr, zs, zr, sys_, syr, sbs, sbr,
            pxs, pxq, pzs, pzq, pys, pyq, pcs, pcq, cxs, cxq, czs_s, czq):
@@ -235,19 +245,21 @@
             czs[w] = acc.astype(BF16)
             cz_copy(w).start()
 
-    product(c)
-    remote(sk.at[o], sk.at[o], sbs, sbr, sibling).wait_recv()
-
     y1 = ysum[...].astype(BF16)
     rest = ysum[...] - y1.astype(F32)
     y2 = rest.astype(BF16)
     y3 = (rest - y2.astype(F32)).astype(BF16)
-    terms = lax.dot_general(
-        jnp.concatenate([y1, y2, y3], axis=0), sk[...].reshape(K, nrow),
-        (((1,), (1,)), ((), ())), preferred_element_type=F32,
-    )
-    terms = (terms[2 * BLOCK:] + terms[BLOCK:2 * BLOCK]) + terms[:BLOCK]
-    pxr[x] = terms * (1.0 / (NX * NZL * nrow))
+    left = jnp.concatenate([y1, y2, y3], axis=0)
+
+    def own_rows(h):
+        terms = lax.dot_general(left, sk[h].reshape(HALF, nrow), (((1,), (1,)), ((), ())),
+                                preferred_element_type=F32)
+        terms = (terms[2 * BLOCK:] + terms[BLOCK:2 * BLOCK]) + terms[:BLOCK]
+        pxr[x, h] = terms * (1.0 / (NX * NZL * nrow))
+
+    own_rows(c)
+    remote(sk.at[o], sk.at[o], sbs, sbr, sibling).wait_recv()
+    own_rows(o)
 
     def px_copy(k):
         r = xpeer(k)
@@ -255,6 +267,7 @@
 
     for k in (2, 1, 3):
         px_copy(k).start()
+    product(c)
     for a in range(2):
         for k in (2, 1, 3):
             cx_copy(2 * c + a, k).start()
@@ -274,7 +287,6 @@
 
     for k in (3, 2, 1):
         pz_copy(k).start()
-    x_sum(2 * c)
     for k in range(1, NZL):
         r = zpeer(k)
         remote(pzr.at[r], pzr.at[r], pzs.at[r], pzq.at[r], zdev(r)).wait_recv()
@@ -286,15 +298,21 @@
 
     for k in far_first:
         py_copy(k).start()
-    x_sum(2 * c + 1)
+    for a in range(2):
+        x_sum(2 * c + a)
     for k in range(1, NY):
         r = ypeer(k)
         remote(cm.at[c, r], cm.at[c, r], pys.at[r], pyq.at[r], device(x, r, z, c)).wait_recv()
     pc_copy = remote(cm.at[c], cm.at[c], pcs, pcq, sibling)
     pc_copy.start()
     remote(cm.at[o], cm.at[o], pcs, pcq, sibling).wait_recv()
-    core = cm[...].reshape(K, K)
-    am[...] = (core + core.T) * 0.5
+    core = jnp.concatenate([cm[:, :, 0].reshape(K, HALF), cm[:, :, 1].reshape(K, HALF)], axis=1)
+    core = (core + core.T) * 0.5
+    on_diagonal = lax.broadcasted_iota(jnp.int32, (K, K), 0) == lax.broadcasted_iota(jnp.int32, (K, K), 1)
+    diagonal = jnp.where(on_diagonal, core, 0.0)
+    across = jnp.sum(diagonal, axis=0, keepdims=True)
+    root[...] = across * lax.rsqrt(across)
+    am[...] = core * lax.rsqrt(jnp.sum(diagonal, axis=1, keepdims=True)) * lax.rsqrt(across)
 
     lane_at = lax.broadcasted_iota(jnp.int32, (SLAB, K), 1)
     sub_at = lax.broadcasted_iota(jnp.int32, (SLAB, K), 0)
@@ -302,7 +320,7 @@
     def slab_step(j, carry):
         start = pl.multiple_of(j * SLAB, SLAB)
         slab = pltpu.roll(am[pl.ds(start, SLAB), :], lax.rem(K - start, K), axis=1)
-        u = pltpu.roll(factor_slab(slab, SLAB, K), start, axis=1)
+        u = pltpu.roll(factor_slab(slab, SLAB, K, held), start, axis=1)
         u = jnp.where(lane_at >= sub_at + start, u, 0.0)
         um[pl.ds(start, SLAB), :] = u
 
@@ -318,7 +336,7 @@
         return carry
 
     lax.fori_loop(0, K // SLAB, slab_step, 0)
-    factor_out[...] = um[...].T
+    factor_out[...] = (um[...] * root[...]).T
 
     acc = zacc[...]
     for k in range(1, NZL):
@@ -355,8 +373,8 @@
         vm((NY, BLOCK, rows_all + HALF), BF16), vm((NY, BLOCK, rows_all + HALF), BF16),
         vm((BLOCK, rows_all + HALF), BF16), vm((BLOCK, rows_all), F32),
         vm((2, NY, BLOCK, rows_all), BF16),
-        vm((NX, BLOCK, K), F32), vm((NZL, BLOCK, K), F32), vm((2, NY, BLOCK, K), F32),
-        vm((K, K), F32), vm((K, K), F32),
+        vm((NX, 2, BLOCK, HALF), F32), vm((NZL, 2, BLOCK, HALF), F32), vm((2, NY, 2, BLOCK, HALF), F32),
+        vm((K, K), F32), vm((K, K), F32), vm((2, 8, 8, HALF), F32), vm((1, K), F32),
         vm((NZL, NX, BLOCK, nvar), F32), vm((NZL, NX, BLOCK, nvar), BF16),
         vm((NZL, NX, BLOCK, nvar), BF16), vm((NZL, BLOCK, nvar), BF16),
         vm((NZL, BLOCK, nvar), BF16), vm((BLOCK, nvar), F32),

time: 65 us -> 62.4 us (0.960)
  Pallas kernels: 62.9 us -> 60.3 us
    pallas_call x1, Pallas kernels: 62.9 us -> 60.3 us  [per_device(): pl.pallas_call(kernel, out_shape=(pltpu.VMEM((BLOCK, nvar), F32), pltpu.V...]
where the time goes in v4:
time: 62.4 us; the launch traced here: 62.3 us
  Pallas kernels  60.3 us (97%)
  local copies, waits for them, and re-layouts  1.36 us (2%)
  between operations  0.64 us (1%)
    pallas_call x1, Pallas kernels, per_device(): pl.pallas_call(kernel, out_shape=(pltpu.VMEM((BLOCK, nvar), F32), pltpu.V...  60.3 us
    unnamed x2, local copies, waits for them, and re-layouts  1.36 us

profile of v4, /device:TPU:1, one launch (start us, length us, event | category | flops | bytes accessed | tf_op | source)
XLA Modules:
  0.0 62.3 jit_solution(15363286676375033446)
XLA Ops:
  0.6 60.3 %sketch.1 = (f32[16,2048]{1,0:T(8,128)S(1)}, f32[256,256]{1,0:T(8,128)S(1)}) custom-call(bf16[768,2048]{1,0:T(8,128)(2,1)} %data.1, bf16[2048,256]{1,0:T(8,128)(2,1)} %test.1), custom_call_target="tpu_custom_call" | custom-call | flops 1610612736 | bytes 4194304 | tf_op jit(solution)/shard_map/sketch/pallas_call | solution.py:388
  61.0 0.7 %copy.6 = f32[2048,16]{0,1:T(8,128)} copy(f32[2048,16]{0,1:T(8,128)S(1)} %bitcast.1) | data formatting | bytes 262144
  61.6 0.7 %copy.7 = f32[256,256]{1,0:T(8,128)} copy(f32[256,256]{1,0:T(8,128)S(1)} %get-tuple-element.7) | data formatting | bytes 524288

commit v5 on v4

--- a/solution.py
+++ b/solution.py
@@ -125,7 +125,7 @@
     part_rows = nrow // 2
     sibling = device(x, y, z, o)
     partner = device(x, y, lax.rem(z + NZL, NZ), c)
-    far_first = (4, 3, 5, 2, 6, 1, 7)
+    far_first = (4, 5, 3, 6, 2, 7, 1)
 
     def ypeer(k):
         return lax.rem(y + k, NY)
@@ -314,28 +314,29 @@
     root[...] = across * lax.rsqrt(across)
     am[...] = core * lax.rsqrt(jnp.sum(diagonal, axis=1, keepdims=True)) * lax.rsqrt(across)
 
-    lane_at = lax.broadcasted_iota(jnp.int32, (SLAB, K), 1)
-    sub_at = lax.broadcasted_iota(jnp.int32, (SLAB, K), 0)
-
-    def slab_step(j, carry):
-        start = pl.multiple_of(j * SLAB, SLAB)
-        slab = pltpu.roll(am[pl.ds(start, SLAB), :], lax.rem(K - start, K), axis=1)
-        u = pltpu.roll(factor_slab(slab, SLAB, K, held), start, axis=1)
-        u = jnp.where(lane_at >= sub_at + start, u, 0.0)
-        um[pl.ds(start, SLAB), :] = u
-
-        @pl.when(j < K // SLAB - 1)
-        def _():
-            am[...] -= lax.dot_general(u, u, (((0,), (0,)), ((), ())),
-                                       precision=HIGHEST, preferred_element_type=F32)
-
-        @pl.when(j < 2)
-        def _():
+    for j in range(K // SLAB):
+        start = j * SLAB
+        low = start // HALF * HALF
+        wide = K - low
+        slab = am[start:start + SLAB, low:]
+        if start > low:
+            slab = pltpu.roll(slab, wide - (start - low), axis=1)
+        u = factor_slab(slab, SLAB, wide, held)
+        if start > low:
+            u = pltpu.roll(u, start - low, axis=1)
+        lane_at = lax.broadcasted_iota(jnp.int32, (SLAB, wide), 1) + low
+        sub_at = lax.broadcasted_iota(jnp.int32, (SLAB, wide), 0) + start
+        u = jnp.where(lane_at >= sub_at, u, 0.0)
+        um[start:start + SLAB, low:] = u
+        if low:
+            um[start:start + SLAB, :low] = jnp.zeros((SLAB, low), F32)
+        if start + SLAB < K:
+            update = lax.dot_general(u, u, (((0,), (0,)), ((), ())),
+                                     precision=HIGHEST, preferred_element_type=F32)
+            am[start + SLAB:, low:] -= update[start + SLAB - low:, :]
+        if j < 2:
             x_sum(2 * o + j)
 
-        return carry
-
-    lax.fori_loop(0, K // SLAB, slab_step, 0)
     factor_out[...] = (um[...] * root[...]).T
 
     acc = zacc[...]

time: 62.4 us -> 61.7 us (0.989)
  Pallas kernels: 60.3 us -> 59.6 us
    pallas_call x1, Pallas kernels: 60.3 us -> 59.6 us  [per_device(): pl.pallas_call(kernel, out_shape=(pltpu.VMEM((BLOCK, nvar), F32), pltpu.V...]
where the time goes in v5:
time: 61.7 us; the launch traced here: 61.6 us
  Pallas kernels  59.6 us (97%)
  local copies, waits for them, and re-layouts  1.36 us (2%)
  between operations  0.64 us (1%)
    pallas_call x1, Pallas kernels, per_device(): pl.pallas_call(kernel, out_shape=(pltpu.VMEM((BLOCK, nvar), F32), pltpu.V...  59.6 us
    unnamed x2, local copies, waits for them, and re-layouts  1.36 us

profile of v5, /device:TPU:1, one launch (start us, length us, event | category | flops | bytes accessed | tf_op | source)
XLA Modules:
  0.0 61.6 jit_solution(12051668585551516296)
XLA Ops:
  0.6 59.6 %sketch.1 = (f32[16,2048]{1,0:T(8,128)S(1)}, f32[256,256]{1,0:T(8,128)S(1)}) custom-call(bf16[768,2048]{1,0:T(8,128)(2,1)} %data.1, bf16[2048,256]{1,0:T(8,128)(2,1)} %test.1), custom_call_target="tpu_custom_call" | custom-call | flops 1610612736 | bytes 4194304 | tf_op jit(solution)/shard_map/sketch/pallas_call | solution.py:389
  60.3 0.7 %copy.6 = f32[2048,16]{0,1:T(8,128)} copy(f32[2048,16]{0,1:T(8,128)S(1)} %bitcast.1) | data formatting | bytes 262144
  60.9 0.7 %copy.7 = f32[256,256]{1,0:T(8,128)} copy(f32[256,256]{1,0:T(8,128)S(1)} %get-tuple-element.7) | data formatting | bytes 524288

commit v6 on v5

--- a/solution.py
+++ b/solution.py
@@ -184,7 +184,7 @@
         y_copy(r).start()
 
     total = part[c, pl.ds(pl.multiple_of(y * BLOCK, BLOCK), BLOCK), :]
-    for k in range(1, NY):
+    for k in reversed(far_first):
         r = ypeer(k)
         remote(q.at[r], yrecv.at[r], ys.at[r], yr.at[r], device(x, r, z, c)).wait_recv()
         total = total + decode(yrecv[r])
@@ -298,8 +298,7 @@
 
     for k in far_first:
         py_copy(k).start()
-    for a in range(2):
-        x_sum(2 * c + a)
+    x_sum(2 * c)
     for k in range(1, NY):
         r = ypeer(k)
         remote(cm.at[c, r], cm.at[c, r], pys.at[r], pyq.at[r], device(x, r, z, c)).wait_recv()
@@ -334,8 +333,11 @@
             update = lax.dot_general(u, u, (((0,), (0,)), ((), ())),
                                      precision=HIGHEST, preferred_element_type=F32)
             am[start + SLAB:, low:] -= update[start + SLAB - low:, :]
-        if j < 2:
-            x_sum(2 * o + j)
+        if j == 0:
+            x_sum(2 * c + 1)
+            x_sum(2 * o)
+        if j == 1:
+            x_sum(2 * o + 1)
 
     factor_out[...] = (um[...] * root[...]).T
 

time: 61.7 us -> 61.8 us (level)
  no operation moved by 1% of the time
where the time goes in v6:
time: 61.8 us; the launch traced here: 61.7 us
  Pallas kernels  59.7 us (97%)
  local copies, waits for them, and re-layouts  1.36 us (2%)
  between operations  0.64 us (1%)
    pallas_call x1, Pallas kernels, per_device(): pl.pallas_call(kernel, out_shape=(pltpu.VMEM((BLOCK, nvar), F32), pltpu.V...  59.7 us
    unnamed x2, local copies, waits for them, and re-layouts  1.36 us

profile of v6, /device:TPU:1, one launch (start us, length us, event | category | flops | bytes accessed | tf_op | source)
XLA Modules:
  0.0 61.7 jit_solution(14749372236440760193)
XLA Ops:
  0.6 59.7 %sketch.1 = (f32[16,2048]{1,0:T(8,128)S(1)}, f32[256,256]{1,0:T(8,128)S(1)}) custom-call(bf16[768,2048]{1,0:T(8,128)(2,1)} %data.1, bf16[2048,256]{1,0:T(8,128)(2,1)} %test.1), custom_call_target="tpu_custom_call" | custom-call | flops 1610612736 | bytes 4194304 | tf_op jit(solution)/shard_map/sketch/pallas_call | solution.py:391
  60.3 0.7 %copy.6 = f32[2048,16]{0,1:T(8,128)} copy(f32[2048,16]{0,1:T(8,128)S(1)} %bitcast.1) | data formatting | bytes 262144
  61.0 0.7 %copy.7 = f32[256,256]{1,0:T(8,128)} copy(f32[256,256]{1,0:T(8,128)S(1)} %get-tuple-element.7) | data formatting | bytes 524288
